TPU v7x, 32 devices: a whole 2x2x4 slice. The times are simulated.
32 devices in a mesh: replica: 2 (over y), adapter: 4 (over z), tensor: 4 (over x, core).
Axes of the slice: x: 2, y: 2, z: 4, core: 2. Of those that a mesh axis runs over, the one named last changes fastest.
Arguments:
- hidden: bfloat16 [512, 4, 8192], P(('replica', 'adapter'), None, 'tensor'), parts along dimension 0, may hold values from -6 to 6
- unrotated_queries: bfloat16 [512, 4, 8192], P(('replica', 'adapter'), None, 'tensor'), parts along dimension 0, may hold values from -6 to 6
- adapter_ids: int32 [512], P(('replica', 'adapter')), parts along dimension 0, may hold values from 0 to 31, as said below
- adapter_home: int32 [64], P('replica'), parts along dimension 0, may hold values from 0 to 31, as said below
- reduce_matrices: bfloat16 [32, 8192, 64], P('adapter', 'tensor'), may hold values from -0.0625 to 0.0625
- expand_matrices: bfloat16 [32, 64, 8192], P('adapter', None, 'tensor'), may hold values from -0.75 to 0.75
- correction_gain_table: float32 [32], P('adapter'), may hold values from 0.25 to 2
- key_cache: bfloat16 [512, 8, 128, 128], P(('replica', 'adapter'), 'tensor'), parts along dimension 0, may hold values from -400 to 400
- value_cache: bfloat16 [512, 8, 128, 128], P(('replica', 'adapter'), 'tensor'), parts along dimension 0, may hold values from -6 to 6
- new_keys: bfloat16 [512, 4, 8, 128], P(('replica', 'adapter'), None, 'tensor'), parts along dimension 0, may hold values from -6 to 6
- new_values: bfloat16 [512, 4, 8, 128], P(('replica', 'adapter'), None, 'tensor'), parts along dimension 0, may hold values from -6 to 6
- cache_len: int32 [512], P(('replica', 'adapter')), parts along dimension 0, may hold values from 2 to 128
Outputs:
- attended: bfloat16 [512, 4, 8192], P(('replica', 'adapter'), None, 'tensor'), parts along dimension 0
There are 2 independent parts, one for each index of `replica`. A program takes and returns all parts, laid end to end along the dimension named above; an argument that names none is the same for every part. Nothing has to cross between parts.
Inputs may be any that keep to these rules, and one draw needn't show every extreme that they name: `adapter_ids`: of the 64 requests of one index of adapter, at most 32 use adapters homed on any one index, and in every draw some index receives exactly 32 from every index. `adapter_home`: A permutation from adapter to home slot; slot s lies on index s // 8 of adapter, at its local slot s % 8.
All inputs are finite; a program needn't handle non-finite values.
Results may differ from a plain program's by a relative error of at most 0.0093.
Values may be sent and summed in bfloat16 or wider, within the bound.
A program may use at most 128 MiB of HBM per device.

v0:
```python
import jax
import jax.numpy as jnp
from jax import lax
from jax.sharding import PartitionSpec as P

rope_theta = 500000.0


def rotate(query, lengths):
    head_dim = query.shape[-1]
    half_dim = head_dim // 2
    frequency = rope_theta ** (-2.0 * jnp.arange(half_dim, dtype=jnp.float32) / head_dim)
    offsets = lengths[:, None] + jnp.arange(query.shape[1], dtype=jnp.int32)[None, :]
    angles = offsets.astype(jnp.float32)[:, :, None] * frequency[None, None, :]
    cos_part = jnp.concatenate([jnp.cos(angles), jnp.cos(angles)], axis=-1)[:, :, None, :]
    sin_part = jnp.concatenate([jnp.sin(angles), jnp.sin(angles)], axis=-1)[:, :, None, :]
    turned = jnp.concatenate([-query[..., half_dim:], query[..., :half_dim]], axis=-1)
    return query * cos_part + turned * sin_part


def attend(query, key_block, value_block, fresh_keys, fresh_values, lengths):
    batch_size, iteration_total, head_count, head_dim = query.shape
    kv_local = key_block.shape[1]
    context = key_block.shape[2]
    grouped = query.reshape(batch_size, iteration_total, kv_local, head_count // kv_local, head_dim)
    scaling = head_dim ** (-0.5)
    old_scores = (
        jnp.einsum("bpkgd,bktd->bpkgt", grouped, key_block, preferred_element_type=jnp.float32)
        * scaling
    )
    new_scores = (
        jnp.einsum("bpkgd,bqkd->bpkgq", grouped, fresh_keys, preferred_element_type=jnp.float32)
        * scaling
    )
    old_valid = (jnp.arange(context, dtype=jnp.int32)[None, :] < lengths[:, None])[
        :, None, None, None, :
    ]
    new_valid = (jnp.arange(iteration_total)[None, :] <= jnp.arange(iteration_total)[:, None])[
        None, :, None, None, :
    ]
    old_scores = jnp.where(old_valid, old_scores, -jnp.inf)
    new_scores = jnp.where(new_valid, new_scores, -jnp.inf)
    row_top = jnp.maximum(
        jnp.max(old_scores, axis=-1, keepdims=True), jnp.max(new_scores, axis=-1, keepdims=True)
    )
    old_exp = jnp.exp(old_scores - row_top)
    new_exp = jnp.exp(new_scores - row_top)
    row_total = jnp.sum(old_exp, axis=-1, keepdims=True) + jnp.sum(new_exp, axis=-1, keepdims=True)
    old_weights = (old_exp / row_total).astype(jnp.bfloat16)
    new_weights = (new_exp / row_total).astype(jnp.bfloat16)
    accumulated_total = jnp.einsum(
        "bpkgt,bktd->bpkgd", old_weights, value_block, preferred_element_type=jnp.float32
    )
    accumulated_total = accumulated_total + jnp.einsum(
        "bpkgq,bqkd->bpkgd", new_weights, fresh_values, preferred_element_type=jnp.float32
    )
    return accumulated_total.reshape(batch_size, iteration_total, head_count * head_dim).astype(
        jnp.bfloat16
    )


def shrink_rows(request_group, labels, reduce_matrices):
    row_order = jnp.argsort(labels, stable=True)
    slot_range = jnp.arange(reduce_matrices.shape[0], dtype=jnp.int32)
    group_sizes = jnp.sum((labels[:, None] == slot_range[None, :]).astype(jnp.int32), axis=0)
    partial_sum = lax.ragged_dot(
        request_group[row_order], reduce_matrices, group_sizes, preferred_element_type=jnp.float32
    )
    return (partial_sum, row_order, group_sizes)


def expand_rows(
    accumulated_total, row_order, group_sizes, labels, expand_matrices, correction_gain_table
):
    sorted_labels = labels[row_order]
    slot_range = jnp.arange(expand_matrices.shape[0], dtype=jnp.int32)
    picked = sorted_labels[:, None] == slot_range[None, :]
    scales = jnp.sum(jnp.where(picked, correction_gain_table[None, :], 0.0), axis=1)
    shrunk = (accumulated_total * scales[:, None]).astype(jnp.bfloat16)
    expanded = lax.ragged_dot(
        shrunk, expand_matrices, group_sizes, preferred_element_type=jnp.float32
    ).astype(jnp.bfloat16)
    return jnp.zeros_like(expanded).at[row_order].set(expanded)


def per_device(
    hidden,
    unrotated_queries,
    adapter_ids,
    adapter_home,
    reduce_matrices,
    expand_matrices,
    correction_gain_table,
    key_cache,
    value_cache,
    new_keys,
    new_values,
    cache_len,
):
    accelerator_list = lax.axis_size("adapter")
    requests, iteration_total, embedding_dimension = hidden.shape
    slots_dev = reduce_matrices.shape[0]
    maximum_load = max(2, (2 * requests + accelerator_list - 1) // accelerator_list)
    table_size = adapter_home.shape[0]
    matches = adapter_ids[:, None] == jnp.arange(table_size, dtype=jnp.int32)[None, :]
    home_slot = jnp.sum(jnp.where(matches, adapter_home[None, :], 0), axis=1)
    target = home_slot // slots_dev
    local_slot = home_slot % slots_dev
    onehot = (target[:, None] == jnp.arange(accelerator_list, dtype=jnp.int32)[None, :]).astype(
        jnp.int32
    )
    before = jnp.cumsum(onehot, axis=0) - onehot
    row_rank = jnp.sum(before * onehot, axis=1)
    resident_position = target * maximum_load + row_rank
    outgoing = (
        jnp.zeros(
            (accelerator_list * maximum_load, iteration_total, embedding_dimension), jnp.bfloat16
        )
        .at[resident_position]
        .set(hidden)
    )
    outgoing = outgoing.reshape(
        accelerator_list, maximum_load, iteration_total, embedding_dimension
    )
    labels = (
        jnp.zeros((accelerator_list * maximum_load,), jnp.int32)
        .at[resident_position]
        .set(local_slot)
        .reshape(accelerator_list, maximum_load)
    )
    arrived, arrived_labels = (
        lax.all_to_all(outgoing, "adapter", split_axis=0, concat_axis=0, tiled=True),
        lax.all_to_all(labels, "adapter", split_axis=0, concat_axis=0, tiled=True),
    )
    flat_labels = jnp.repeat(arrived_labels.reshape(-1), iteration_total)
    partial_sum, row_order, group_sizes = shrink_rows(
        arrived.reshape(-1, embedding_dimension), flat_labels, reduce_matrices
    )
    accumulated_total = lax.psum(partial_sum, "tensor")
    expanded = expand_rows(
        accumulated_total,
        row_order,
        group_sizes,
        flat_labels,
        expand_matrices,
        correction_gain_table,
    )
    returning_parts = lax.all_to_all(
        expanded.reshape(accelerator_list, maximum_load, iteration_total, embedding_dimension),
        "adapter",
        split_axis=0,
        concat_axis=0,
        tiled=True,
    )
    low_rank_correction = returning_parts.reshape(
        accelerator_list * maximum_load, iteration_total, embedding_dimension
    )[resident_position]
    head_dim = key_cache.shape[3]
    merged_output = unrotated_queries.astype(jnp.float32) + low_rank_correction.astype(jnp.float32)
    query = rotate(
        merged_output.reshape(requests, iteration_total, embedding_dimension // head_dim, head_dim),
        cache_len,
    ).astype(jnp.bfloat16)
    return attend(query, key_cache, value_cache, new_keys, new_values, cache_len)


def solution(mesh):
    in_specs = (
        P(("replica", "adapter"), None, "tensor"),
        P(("replica", "adapter"), None, "tensor"),
        P(("replica", "adapter")),
        P("replica"),
        P("adapter", "tensor", None),
        P("adapter", None, "tensor"),
        P("adapter"),
        P(("replica", "adapter"), "tensor", None, None),
        P(("replica", "adapter"), "tensor", None, None),
        P(("replica", "adapter"), None, "tensor", None),
        P(("replica", "adapter"), None, "tensor", None),
        P(("replica", "adapter")),
    )
    out_specs = P(("replica", "adapter"), None, "tensor")
    return jax.shard_map(
        per_device, mesh=mesh, in_specs=in_specs, out_specs=out_specs, check_vma=False
    )
```

profile of v0, /device:TPU:0, one launch (start us, length us, event | category | flops | bytes accessed | tf_op | source)
XLA Modules:
  0.0 233.3 jit_solution(15602018127308885603)
XLA Ops:
  6.5 0.0 copy-start
  6.5 0.9 select_reduce_fusion.2
  7.4 0.1 fusion.27
  7.5 0.1 reduce_window_sum.11
  7.6 0.2 select_reduce_fusion
  7.8 0.8 scatter_custom_fusion
  8.6 0.7 all_to_all.12
  9.2 6.3 %all-to-all-start = ((s32[4,1,32]{2,1,0:T(1,128)}), s32[4,1,32]{2,1,0:T(1,128)S(1)}, u32[]{:S(2)}, u32[]{:S(2)}) async-start(s32[4,1,32]{2,1,0:T(1,128)} %bitcast.3), calls=%async_computation | async-start | bytes 4096 | tf_op jit(solution)/shard_map/all_to_all | solution.py:133
  15.5 2.4 %broadcast_in_dim.65 = bf16[128,4,2048]{2,1,0:T(4,128)(2,1)} broadcast(bf16[]{:T(256)} %constant.23.clone.1), dimensions={} | broadcast | bytes 2097154 | tf_op jit(solution)/shard_map/broadcast_in_dim | solution.py:116
  17.9 0.0 copy-done.4
  17.9 8.1 %scatter_fusion = bf16[128,4,2048]{2,1,0:T(4,128)(2,1)} fusion(bf16[128,4,2048]{2,1,0:T(4,128)(2,1)} %broadcast_in_dim.65, s32[64]{0:T(128)S(1)} %fusion.28, bf16[64,4,2048]{2,1,0:T(4,128)(2,1)S(1)} %copy-done.4), kind=kCustom, calls=%fused_computation.4 | custom fusion | bytes 3145984 | tf_op jit(solution)/shard_map/scatter | solution.py:120
  26.1 0.0 all-to-all-done
  26.1 5.2 %all-to-all-start.1 = ((bf16[4,32,4,2048]{3,2,1,0:T(4,128)(2,1)}), bf16[4,32,4,2048]{3,2,1,0:T(4,128)(2,1)}, u32[]{:S(2)}, u32[]{:S(2)}) async-start(bf16[4,32,4,2048]{3,2,1,0:T(4,128)(2,1)} %bitcast.4), calls=%async_computation.1 | async-start | bytes 4194304 | tf_op jit(solution)/shard_map/all_to_all | solution.py:132
  31.3 0.0 all-reduce.2.cloned.1.call-start
  31.3 0.0 copy-done.3
  31.3 3.2 %copy.33 = bf16[8,2048,64]{2,1,0:T(8,128)(2,1)} copy(bf16[8,2048,64]{1,2,0:T(8,128)(2,1)S(1)} %copy-done.3) | data formatting | bytes 4194304 | tf_op args[4]
  34.5 0.5 broadcast.203
  35.0 0.7 reduce.3
  35.7 0.1 reshape.178
  35.8 0.1 broadcast_in_dim.59
  35.8 0.1 reshape.179
  36.0 3.8 %sort.17 = (s32[512]{0:T(512)}, s32[512]{0:T(512)S(1)}) sort(s32[512]{0:T(512)S(1)} %reshape.179, s32[512]{0:T(512)S(1)} %iota.47), dimensions={0}, to_apply=%region_4.5 | sort | flops 4608 | bytes 8192 | tf_op jit(solution)/shard_map/jit(argsort)/sort | solution.py:63
  39.7 0.6 convert_reduce_fusion
  40.4 1.5 ragged-dot-metadata
  41.9 3.5 %gather_fusion.1 = s32[512]{0:T(512)S(1)} fusion(s32[512]{0:T(512)S(1)} %reshape.179, s32[1024]{0:T(1024)S(1)} %pad_clamp_fusion.1), kind=kCustom, calls=%fused_computation.1 | custom fusion | bytes 6144 | tf_op jit(solution)/shard_map/gather | solution.py:75
  45.4 33.7 %all-to-all-done.1 = bf16[4,32,4,2048]{3,2,1,0:T(4,128)(2,1)} async-done(((bf16[4,32,4,2048]{3,2,1,0:T(4,128)(2,1)}), bf16[4,32,4,2048]{3,2,1,0:T(4,128)(2,1)}, u32[]{:S(2)}, u32[]{:S(2)}) %all-to-all-start.1) | async-done | bytes 2097184 | tf_op jit(solution)/shard_map/all_to_all | solution.py:132
  79.0 2.5 %reshape.181 = bf16[512,2048]{1,0:T(8,128)(2,1)S(1)} reshape(bf16[4,32,4,2048]{3,2,1,0:T(4,128)(2,1)} %all-to-all-done.1) | data formatting | bytes 4194304 | tf_op jit(solution)/shard_map/reshape | solution.py:137
  81.6 3.3 %gather_fusion = bf16[512,2048]{1,0:T(8,128)(2,1)} fusion(bf16[512,2048]{1,0:T(8,128)(2,1)S(1)} %reshape.181, s32[1024]{0:T(1024)S(1)} %pad_clamp_fusion.1), kind=kCustom, calls=%fused_computation | custom fusion | bytes 4196352 | tf_op jit(solution)/shard_map/gather | solution.py:67
  84.9 10.5 %ragged-dot-none.1 = f32[512,64]{1,0:T(8,128)} custom-call(s32[1]{0:T(128)} %get-tuple-element.7, s32[9]{0:T(128)} %get-tuple-element.8, s32[9]{0:T(128)} %get-tuple-element.9, s32[9]{0:T(128)} %get-tuple-element.10, s32[1]{0:T(128)} %get-tuple-element.7, bf16[512,2048]{1,0:T(8,128)(2,1)} %gather_fusion, bf16[8,2048,64]{2,1,0:T(8,128)(2,1)} %copy.33), custom_call_target="tpu_custom_call" | custom-call | flops 134217728 | bytes 4325408 | tf_op jit(solution)/shard_map/ragged_dot_general/ragged-dot-none
  95.4 0.0 all-reduce.2.cloned.1.call-update
  95.5 0.0 copy-done.6
  95.5 0.1 select_reduce_fusion.1
  95.6 31.1 %all-reduce.2.cloned.1.call-done = f32[512,64]{1,0:T(8,128)} async-done(((f32[512,64]{1,0:T(8,128)}), f32[512,64]{1,0:T(8,128)}) %all-reduce.2.cloned.1.call-update) | async-done | bytes 131088 | tf_op jit(solution)/shard_map/psum | solution.py:139
  126.7 1.7 multiply_convert_fusion
  128.4 10.6 %ragged-dot-none = f32[512,2048]{1,0:T(8,128)} custom-call(s32[1]{0:T(128)} %get-tuple-element.7, s32[9]{0:T(128)} %get-tuple-element.8, s32[9]{0:T(128)} %get-tuple-element.9, s32[9]{0:T(128)} %get-tuple-element.10, s32[1]{0:T(128)} %get-tuple-element.7, bf16[512,64]{1,0:T(8,128)(2,1)} %multiply_convert_fusion, bf16[8,64,2048]{2,1,0:T(8,128)(2,1)} %param.17), custom_call_target="tpu_custom_call" | custom-call | flops 134217728 | bytes 6357024 | tf_op jit(solution)/shard_map/ragged_dot_general/ragged-dot-none
  139.1 5.8 %scatter_custom_fusion.2 = bf16[512,2048]{1,0:T(8,128)(2,1)S(1)} fusion(s32[512]{0:T(512)S(1)} %compare_select_fusion, f32[512,2048]{1,0:T(8,128)} %ragged-dot-none, bf16[]{:T(256)} %constant.23.clone.1), kind=kCustom, calls=%fused_computation.23 | custom fusion | flops 1048576 | bytes 6291458 | tf_op jit(solution)/shard_map/scatter | solution.py:83
  144.9 2.2 reshape.182
  147.2 4.7 %all-to-all-start.2 = ((bf16[4,32,4,2048]{3,2,1,0:T(4,128)(2,1)}), bf16[4,32,4,2048]{3,2,1,0:T(4,128)(2,1)S(1)}, u32[]{:S(2)}, u32[]{:S(2)}) async-start(bf16[4,32,4,2048]{3,2,1,0:T(4,128)(2,1)} %reshape.182), calls=%async_computation.2 | async-start | bytes 4194304 | tf_op jit(solution)/shard_map/all_to_all | solution.py:148
  151.9 0.0 copy-done.5
  151.9 0.1 add_convert_fusion.1
  152.0 1.1 multiply_cosine_fusion
  153.1 0.2 pad_maximum_fusion
  153.3 0.1 iota_compare_fusion.1
  153.3 45.6 %all-to-all-done.2 = bf16[4,32,4,2048]{3,2,1,0:T(4,128)(2,1)S(1)} async-done(((bf16[4,32,4,2048]{3,2,1,0:T(4,128)(2,1)}), bf16[4,32,4,2048]{3,2,1,0:T(4,128)(2,1)S(1)}, u32[]{:S(2)}, u32[]{:S(2)}) %all-to-all-start.2) | async-done | bytes 2097184 | tf_op jit(solution)/shard_map/all_to_all | solution.py:148
  198.9 1.4 gather_fusion.2
  200.4 2.9 %convert_add_fusion = f32[32,8,2048]{2,1,0:T(8,128)} fusion(bf16[32,8,2048]{2,1,0:T(8,128)(2,1)S(1)} %bitcast.60, bf16[32,8,2048]{2,1,0:T(8,128)(2,1)} %bitcast.61), kind=kLoop, calls=%fused_computation.22 | loop fusion | flops 1572864 | bytes 4194304 | tf_op jit(solution)/shard_map/add | solution.py:159
  203.3 2.3 reshape.185
  205.6 3.3 %reshape.184 = f32[64,4,2,8,128]{4,3,2,1,0:T(8,128)} reshape(f32[64,4,2048]{2,1,0:T(4,128)} %bitcast.58) | data formatting | bytes 4194304 | tf_op jit(solution)/shard_map/reshape | solution.py:161
  208.9 0.8 fusion.4
  209.7 0.8 copy-done.1
  210.5 0.8 fusion.6
  211.4 1.4 copy-done.2
  212.7 2.5 %bitcast_reduce_fusion = (f32[64,4,2,8]{3,1,2,0:T(4,128)S(1)}, f32[64,2,4,8,128]{4,3,2,1,0:T(8,128)S(1)}) fusion(pred[64,128]{1,0:T(8,128)(4,1)S(1)} %iota_compare_fusion.1, bf16[64,2,128,128]{3,2,1,0:T(8,128)(2,1)S(1)} %copy-done.2, bf16[64,4,2,8,128]{4,3,2,1,0:T(8,128)(2,1)S(1)} %fusion.6), kind=kOutput, calls=%fused_computation.17 | convolution fusion | flops 135786496 | bytes 7364608 | tf_op jit(solution)/shard_map/bpkgd,bktd->bpkgt/dot_general | solution.py:28
  215.2 4.7 %fusion.33 = (f32[64,4,2,8]{3,1,2,0:T(4,128)S(1)}, f32[64,4,2,8,4]{3,4,1,2,0:T(4,128)S(1)}) fusion(bf16[64,4,2,128,1]{3,2,1,0,4:T(2,128)(2,1)S(1)} %bitcast.62, bf16[64,4,2,8,128]{4,3,2,1,0:T(8,128)(2,1)S(1)} %fusion.6, pred[4,4]{1,0:T(4,128)(4,1)S(1)} %iota_compare_fusion.5), kind=kOutput, calls=%fused_computation.83 | convolution fusion | flops 4239360 | bytes 1261584 | tf_op jit(solution)/shard_map/bpkgd,bqkd->bpkgq/dot_general | solution.py:32
  219.9 0.1 max.8
  220.0 0.0 copy-start.7
  220.0 1.0 fusion.22
  221.0 1.4 fusion.10
  222.4 0.1 add.88
  222.5 1.9 fusion
  224.3 0.0 copy-done
  224.3 0.8 fusion.11
  225.2 0.2 copy.48
  225.4 1.1 reshape.241
  (17 shorter events, 0.1 us)
Async XLA Ops:
  6.5 217.8 %copy-start = (bf16[64,4,2,128]{3,2,1,0:T(2,128)(2,1)S(1)}, bf16[64,4,2,128]{3,2,1,0:T(2,128)(2,1)}, u32[]{:S(2)}) copy-start(bf16[64,4,2,128]{3,2,1,0:T(2,128)(2,1)} %param.22) | copy-start | bytes 393220
  6.5 11.4 %copy-start.4 = (bf16[64,4,2048]{2,1,0:T(4,128)(2,1)S(1)}, bf16[64,4,2048]{2,1,0:T(4,128)(2,1)}, u32[]{:S(2)}) copy-start(bf16[64,4,2048]{2,1,0:T(4,128)(2,1)} %param.12) | copy-start | bytes 3145732
  9.2 16.9 %all-to-all-start = ((s32[4,1,32]{2,1,0:T(1,128)}), s32[4,1,32]{2,1,0:T(1,128)S(1)}, u32[]{:S(2)}, u32[]{:S(2)}) async-start(s32[4,1,32]{2,1,0:T(1,128)} %bitcast.3), calls=%async_computation | async-start | bytes 4096 | tf_op jit(solution)/shard_map/all_to_all | solution.py:133
  26.1 5.2 %copy-start.3 = (bf16[8,2048,64]{1,2,0:T(8,128)(2,1)S(1)}, bf16[8,2048,64]{1,2,0:T(8,128)(2,1)}, u32[]{:S(2)}) copy-start(bf16[8,2048,64]{1,2,0:T(8,128)(2,1)} %param.16) | copy-start | bytes 6291460
  26.1 53.0 %all-to-all-start.1 = ((bf16[4,32,4,2048]{3,2,1,0:T(4,128)(2,1)}), bf16[4,32,4,2048]{3,2,1,0:T(4,128)(2,1)}, u32[]{:S(2)}, u32[]{:S(2)}) async-start(bf16[4,32,4,2048]{3,2,1,0:T(4,128)(2,1)} %bitcast.4), calls=%async_computation.1 | async-start | bytes 4194304 | tf_op jit(solution)/shard_map/all_to_all | solution.py:132
  31.3 95.4 %all-reduce.2.cloned.1.call-start = ((), (), s32[]{:S(2)}) async-start(), calls=%async_computation.3 | async-start | bytes 524288 | tf_op jit(solution)/shard_map/psum | solution.py:139
  84.9 10.6 %copy-start.6 = (f32[8]{0:T(128)S(1)}, f32[8]{0:T(128)}, u32[]{:S(2)}) copy-start(f32[8]{0:T(128)} %param.18) | copy-start | bytes 100
  147.2 4.7 %copy-start.5 = (s32[64]{0:T(128)S(1)}, s32[64]{0:T(128)}, u32[]{:S(2)}) copy-start(s32[64]{0:T(128)} %param.23) | copy-start | bytes 772
  147.2 51.7 %all-to-all-start.2 = ((bf16[4,32,4,2048]{3,2,1,0:T(4,128)(2,1)}), bf16[4,32,4,2048]{3,2,1,0:T(4,128)(2,1)S(1)}, u32[]{:S(2)}, u32[]{:S(2)}) async-start(bf16[4,32,4,2048]{3,2,1,0:T(4,128)(2,1)} %reshape.182), calls=%async_computation.2 | async-start | bytes 4194304 | tf_op jit(solution)/shard_map/all_to_all | solution.py:148
  208.9 1.6 copy-start.1
  210.5 2.2 copy-start.2
  212.7 2.5 %copy-start.8 = (bf16[64,4,2,128]{3,2,1,0:T(2,128)(2,1)S(1)}, bf16[64,4,2,128]{3,2,1,0:T(2,128)(2,1)}, u32[]{:S(2)}) copy-start(bf16[64,4,2,128]{3,2,1,0:T(2,128)(2,1)} %param.21) | copy-start | bytes 393220
  220.0 2.5 %copy-start.7 = (bf16[64,2,128,128]{3,2,1,0:T(8,128)(2,1)S(1)}, bf16[64,2,128,128]{3,2,1,0:T(8,128)(2,1)}, u32[]{:S(2)}) copy-start(bf16[64,2,128,128]{3,2,1,0:T(8,128)(2,1)} %param.20) | copy-start | bytes 12582916
Sparse Core Ops, SparseCore 0:
  95.6 31.0 all-reduce.1
where the time goes:
time: 235 us; the launch traced here: 233 us
  waiting for transfers between devices  110 us (47%)
  local copies, waits for them, and re-layouts  38.1 us (16%)
  Pallas kernels  22.7 us (10%)
  other arithmetic  22.5 us (10%)
  starting transfers between devices  16.2 us (7%)
  between operations  13.6 us (6%)
  matrix products  9.85 us (4%)
    all_to_all x1, waiting for transfers between devices, per_device(): lax.all_to_all(expanded.reshape(accelerator_list, maximum_load, iteration...  45.6 us
    all_to_all x1, waiting for transfers between devices, per_device(): lax.all_to_all(outgoing, 'adapter', split_axis=0, concat_axis=0, tiled=True)  33.7 us
    psum x1, waiting for transfers between devices, per_device(): accumulated_total = lax.psum(partial_sum, 'tensor')  31.1 us
    another operation x2, Pallas kernels  21.2 us
    scatter x1, local copies, waits for them, and re-layouts, per_device(): outgoing = jnp.zeros((accelerator_list * maximum_load, iteration_total, e...  8.14 us
    all_to_all x1, starting transfers between devices, per_device(): lax.all_to_all(labels, 'adapter', split_axis=0, concat_axis=0, tiled=True)  6.32 us
    scatter x1, other arithmetic, expand_rows(): return jnp.zeros_like(expanded).at[row_order].set(expanded)  5.83 us
    reshape x2, local copies, waits for them, and re-layouts, per_device(): merged_output.reshape(requests, iteration_total, embedding_dimension // h...  5.63 us
  transfers between devices with their start and end apart: 4, of which 3 were waited for; matrix products, arithmetic and copies ran while one was open for 11% of the time, Pallas kernels for 1%

commit v1 on v0

v1 whole, which is shorter than its diff:
```python
import functools

import jax
import jax.numpy as jnp
from jax import lax
from jax.experimental import pallas as pl
from jax.experimental.pallas import tpu as pltpu
from jax.sharding import PartitionSpec as P

rope_theta = 500000.0
MESH = pl.DeviceIdType.MESH


def nt_dot(a, b):
    return lax.dot_general(a, b, (((1,), (1,)), ((), ())), preferred_element_type=jnp.float32)


def log2(n):
    bits = n.bit_length() - 1
    assert 1 << bits == n
    return bits


def kernel(
    dims,
    len_ref,
    pos_ref,
    pos_col_ref,
    slot_ref,
    gain_ref,
    hidden_hbm,
    uq_hbm,
    down_hbm,
    up_hbm,
    key_hbm,
    value_hbm,
    fresh_key_hbm,
    fresh_value_hbm,
    cos_ref,
    sin_ref,
    out_ref,
    hidden,
    uq,
    down,
    up,
    keys,
    values,
    outgoing,
    arrived,
    labels_out,
    labels_in,
    partial,
    returning,
    returned,
    rows,
    local_sems,
    out_send,
    out_recv,
    label_send,
    label_recv,
    part_send,
    part_recv,
    back_send,
    back_recv,
):
    n, tensors, chunks, cap, reqs, positions, context = dims
    per = positions // chunks
    block = per * cap
    total = n * block
    half = total // 2
    width = hidden.shape[-1]
    heads = width // 128
    kv = keys.shape[1]
    group = heads // kv
    row_count = positions * heads
    replica = lax.axis_index("replica")
    me = lax.axis_index("adapter")
    column = lax.axis_index("tensor")

    def adapter_peer(k):
        return (replica, lax.rem(me + k + n, n), column)

    def tensor_peer(k):
        return (replica, me, lax.rem(column + k, tensors))

    loads = [
        pltpu.make_async_copy(hidden_hbm, hidden, local_sems.at[0]),
        pltpu.make_async_copy(down_hbm, down, local_sems.at[1]),
        pltpu.make_async_copy(up_hbm, up, local_sems.at[2]),
        pltpu.make_async_copy(uq_hbm, uq, local_sems.at[3]),
        pltpu.make_async_copy(key_hbm, keys.at[:, :, pl.ds(0, context), :], local_sems.at[4]),
        pltpu.make_async_copy(value_hbm, values.at[:, :, pl.ds(0, context), :], local_sems.at[5]),
        pltpu.make_async_copy(
            fresh_key_hbm, keys.at[:, :, pl.ds(context, 16), :], local_sems.at[6]
        ),
        pltpu.make_async_copy(
            fresh_value_hbm, values.at[:, :, pl.ds(context, 16), :], local_sems.at[7]
        ),
    ]
    for load in loads:
        load.start()

    barrier = pltpu.get_barrier_semaphore()
    for k in range(1, n):
        pl.semaphore_signal(barrier, inc=1, device_id=adapter_peer(k), device_id_type=MESH)
    for k in range(1, tensors):
        pl.semaphore_signal(barrier, inc=1, device_id=tensor_peer(k), device_id_type=MESH)

    def out_copy(c, k):
        return pltpu.make_async_remote_copy(
            outgoing.at[c, k], arrived.at[c, k], out_send.at[c, k], out_recv.at[c, k],
            device_id=adapter_peer(k), device_id_type=MESH,
        )

    def label_copy(k):
        return pltpu.make_async_remote_copy(
            labels_out.at[k], labels_in.at[k], label_send.at[k], label_recv.at[k],
            device_id=adapter_peer(k), device_id_type=MESH,
        )

    def part_copy(c, k):
        return pltpu.make_async_remote_copy(
            partial.at[c, 0], partial.at[c, k], part_send.at[c, k], part_recv.at[c, k],
            device_id=tensor_peer(k), device_id_type=MESH,
        )

    def back_copy(c, k):
        return pltpu.make_async_remote_copy(
            returning.at[c, k], returned.at[c, k], back_send.at[c, k], back_recv.at[c, k],
            device_id=adapter_peer(-k), device_id_type=MESH,
        )

    def pick(shape, row_axis, pos):
        row = lax.broadcasted_iota(jnp.int32, shape, row_axis)
        col = lax.broadcasted_iota(jnp.int32, shape, 1 - row_axis)
        peer = row >> log2(block)
        row_pos = (row >> log2(cap)) & (per - 1)
        slot = row & (cap - 1)
        return (pos == peer * cap + slot) & (row_pos == (col >> log2(reqs)))

    forward = pick((total, per * reqs), 0, pos_ref[...])
    label_rows = jnp.sum(jnp.where(forward, slot_ref[...], 0), axis=1, keepdims=True)
    label_rows = jnp.broadcast_to(label_rows, (total, 128)).reshape(n, block, 128)
    labels_out[...] = label_rows
    labels_in[0] = label_rows[0]
    forward = jnp.where(forward, 1.0, 0.0).astype(jnp.bfloat16)

    loads[0].wait()
    pl.semaphore_wait(barrier, n - 1 + tensors - 1)
    for k in range(1, n):
        label_copy(k).start()

    def dispatch(c, _):
        source = hidden[pl.ds(pl.multiple_of(c * per * reqs, per * reqs), per * reqs), :]
        sent = jnp.dot(forward, source, preferred_element_type=jnp.float32)
        sent = sent.astype(jnp.bfloat16).reshape(n, block, width)
        outgoing[c] = sent
        arrived[c, 0] = sent[0]
        for k in range(1, n):
            out_copy(c, k).start()
        return 0

    lax.fori_loop(0, chunks, dispatch, 0)
    for k in range(1, n):
        label_copy(k).wait()
    loads[1].wait()
    loads[2].wait()

    def work(c, _):
        for k in range(1, n):
            out_copy(c, k).wait_recv()
        label = labels_in[...].reshape(total, 128)
        lane = lax.broadcasted_iota(jnp.int32, (total, 128), 1)
        odd = jnp.where(lane >= 64, 1, 0)
        product = nt_dot(arrived[c].reshape(total, width), down[...])
        kept = jnp.zeros((total, 128), jnp.float32)
        groups = down.shape[0] // 128
        for j in range(groups):
            kept = kept + jnp.where(label == 2 * j + odd, product[:, j * 128 : (j + 1) * 128], 0.0)
        kept = kept + pltpu.roll(kept, 64, 1)
        low = lax.broadcasted_iota(jnp.int32, (half, 128), 1) < 64
        partial[c, 0] = jnp.where(low, kept[:half], kept[half:])
        for k in range(1, tensors):
            part_copy(c, k).start()
        for k in range(1, tensors):
            part_copy(c, k).wait()
        summed = partial[c, 0]
        for k in range(1, tensors):
            summed = summed + partial[c, k]
        turned = pltpu.roll(summed, 64, 1)
        both = jnp.concatenate(
            [jnp.where(low, summed, turned), jnp.where(low, turned, summed)], axis=0
        )
        pieces = []
        for j in range(groups):
            scaled = both * gain_ref[:, j * 128 : (j + 1) * 128]
            pieces.append(jnp.where(label == 2 * j + odd, scaled, 0.0).astype(jnp.bfloat16))
        shrunk = jnp.concatenate(pieces, axis=1)
        expanded = jnp.dot(shrunk, up[...], preferred_element_type=jnp.float32)
        expanded = expanded.astype(jnp.bfloat16).reshape(n, block, width)
        returning[c] = expanded
        returned[c, 0] = expanded[0]
        for k in range(1, n):
            back_copy(c, k).start()
        return 0

    lax.fori_loop(0, chunks, work, 0)

    backward = pick((per * reqs, total), 1, pos_col_ref[...])
    backward = jnp.where(backward, 1.0, 0.0).astype(jnp.bfloat16)
    loads[3].wait()

    def combine(c, _):
        for k in range(1, n):
            back_copy(c, k).wait_recv()
        span = pl.ds(pl.multiple_of(c * per * reqs, per * reqs), per * reqs)
        delta = jnp.dot(
            backward, returned[c].reshape(total, width), preferred_element_type=jnp.float32
        )
        merged = uq[span, :].astype(jnp.float32) + delta
        cosine = cos_ref[span, :]
        sine = sin_ref[span, :]
        for h in range(heads):
            part = merged[:, h * 128 : (h + 1) * 128]
            part = part * cosine + pltpu.roll(part, 64, 1) * sine
            for i in range(per):
                first = (h // group) * positions * group + (c * per + i) * group + h % group
                rows[pl.ds(first, reqs, stride=row_count), :] = part[i * reqs : (i + 1) * reqs]
        return 0

    lax.fori_loop(0, chunks, combine, 0)
    for load in loads[4:]:
        load.wait()

    queries = positions * group
    lane = lax.broadcasted_iota(jnp.int32, (queries, context + 16), 1)
    at = lax.broadcasted_iota(jnp.int32, (queries, context + 16), 0) >> log2(group)
    new_valid = (lane >= context) & (lane - context <= at)
    scaling = 128 ** (-0.5)

    def attend(r):
        old_valid = lane < jnp.minimum(len_ref[r], context)
        valid = old_valid | new_valid
        for g in range(kv):
            span = pl.ds(pl.multiple_of(r * row_count + g * queries, queries), queries)
            query = rows[span, :].astype(jnp.bfloat16)
            scores = nt_dot(query, keys[r, g]) * scaling
            scores = jnp.where(valid, scores, -jnp.inf)
            top = jnp.max(scores, axis=1, keepdims=True)
            weights = jnp.exp(scores - top)
            weights = weights / jnp.sum(weights, axis=1, keepdims=True)
            rows[span, :] = jnp.dot(
                weights.astype(jnp.bfloat16), values[r, g], preferred_element_type=jnp.float32
            )

    def attend_some(b, _):
        for i in range(4):
            attend(b * 4 + i)
        return 0

    lax.fori_loop(0, reqs // 4, attend_some, 0)

    def finish(p, _):
        for h in range(heads):
            first = (h // group) * positions * group + p * group + h % group
            part = rows[pl.ds(first, reqs, stride=row_count), :]
            out_ref[p, :, h * 128 : (h + 1) * 128] = part.astype(jnp.bfloat16)
        return 0

    lax.fori_loop(0, positions, finish, 0)

    for k in range(1, n):
        def drain(c, _):
            out_copy(c, k).wait_send()
            back_copy(c, k).wait_send()
            return 0

        lax.fori_loop(0, chunks, drain, 0)


def per_device(
    hidden,
    unrotated_queries,
    adapter_ids,
    adapter_home,
    reduce_matrices,
    expand_matrices,
    correction_gain_table,
    key_cache,
    value_cache,
    new_keys,
    new_values,
    cache_len,
):
    n = lax.axis_size("adapter")
    tensors = lax.axis_size("tensor")
    me = lax.axis_index("adapter")
    reqs, positions, width = hidden.shape
    slots_dev, _, rank = reduce_matrices.shape
    kv, context, head_dim = key_cache.shape[1:]
    assert rank == 64 and head_dim == 128 and slots_dev % 2 == 0
    cap = max(2, (2 * reqs + n - 1) // n)
    chunks = max(1, min(positions, positions * cap // 16))
    per = positions // chunks
    block = per * cap
    total = n * block
    matches = adapter_ids[:, None] == jnp.arange(adapter_home.shape[0], dtype=jnp.int32)[None, :]
    home_slot = jnp.sum(jnp.where(matches, adapter_home[None, :], 0), axis=1)
    hop = lax.rem(home_slot // slots_dev - me + n, n)
    local_slot = home_slot % slots_dev
    order = jnp.arange(reqs, dtype=jnp.int32)
    earlier = (hop[:, None] == hop[None, :]) & (order[None, :] < order[:, None])
    pos = hop * cap + jnp.sum(earlier.astype(jnp.int32), axis=1)
    pos = jnp.tile(pos, per)
    slot_row = jnp.tile(local_slot, per)[None, :]
    gain_row = jnp.repeat(correction_gain_table, rank)[None, :]

    half = head_dim // 2
    frequency = rope_theta ** (-2.0 * jnp.arange(half, dtype=jnp.float32) / head_dim)
    offsets = cache_len[None, :] + jnp.arange(positions, dtype=jnp.int32)[:, None]
    angles = offsets.astype(jnp.float32)[:, :, None] * frequency[None, None, :]
    cosine, sine = jnp.cos(angles), jnp.sin(angles)
    cosine = jnp.concatenate([cosine, cosine], axis=-1).reshape(positions * reqs, head_dim)
    sine = jnp.concatenate([-sine, sine], axis=-1).reshape(positions * reqs, head_dim)

    def by_position(array):
        return array.transpose(1, 0, 2).reshape(positions * reqs, width)

    def fresh(array):
        return jnp.pad(array.transpose(0, 2, 1, 3), ((0, 0), (0, 0), (0, 16 - positions), (0, 0)))

    down = reduce_matrices.transpose(0, 2, 1).reshape(slots_dev * rank, width)
    up = expand_matrices.reshape(slots_dev * rank, width)
    dims = (n, tensors, chunks, cap, reqs, positions, context)
    bf16, f32 = jnp.bfloat16, jnp.float32
    dma = pltpu.SemaphoreType.DMA
    vmem = pl.BlockSpec(memory_space=pltpu.VMEM)
    whole = pl.BlockSpec(memory_space=pl.ANY)
    attended = pl.pallas_call(
        functools.partial(kernel, dims),
        out_shape=jax.ShapeDtypeStruct((positions, reqs, width), bf16),
        in_specs=[pl.BlockSpec(memory_space=pltpu.SMEM)] + [vmem] * 4 + [whole] * 8 + [vmem] * 2,
        out_specs=vmem,
        scratch_shapes=[
            pltpu.VMEM((positions * reqs, width), bf16),
            pltpu.VMEM((positions * reqs, width), bf16),
            pltpu.VMEM(down.shape, bf16),
            pltpu.VMEM(up.shape, bf16),
            pltpu.VMEM((reqs, kv, context + 16, head_dim), bf16),
            pltpu.VMEM((reqs, kv, context + 16, head_dim), bf16),
            pltpu.VMEM((chunks, n, block, width), bf16),
            pltpu.VMEM((chunks, n, block, width), bf16),
            pltpu.VMEM((n, block, 128), jnp.int32),
            pltpu.VMEM((n, block, 128), jnp.int32),
            pltpu.VMEM((chunks, tensors, total // 2, 128), f32),
            pltpu.VMEM((chunks, n, block, width), bf16),
            pltpu.VMEM((chunks, n, block, width), bf16),
            pltpu.VMEM((reqs * positions * width // head_dim, head_dim), f32),
            dma((8,)),
            dma((chunks, n)),
            dma((chunks, n)),
            dma((n,)),
            dma((n,)),
            dma((chunks, tensors)),
            dma((chunks, tensors)),
            dma((chunks, n)),
            dma((chunks, n)),
        ],
        compiler_params=pltpu.CompilerParams(
            collective_id=0, has_side_effects=True, vmem_limit_bytes=56 * 1024 * 1024
        ),
        cost_estimate=pl.CostEstimate(flops=3 << 30, bytes_accessed=16 << 20, transcendentals=0),
    )(
        cache_len,
        pos[None, :],
        pos[:, None],
        slot_row,
        gain_row,
        by_position(hidden),
        by_position(unrotated_queries),
        down,
        up,
        key_cache,
        value_cache,
        fresh(new_keys),
        fresh(new_values),
        cosine,
        sine,
    )
    return attended.transpose(1, 0, 2)


def solution(mesh):
    in_specs = (
        P(("replica", "adapter"), None, "tensor"),
        P(("replica", "adapter"), None, "tensor"),
        P(("replica", "adapter")),
        P("replica"),
        P("adapter", "tensor", None),
        P("adapter", None, "tensor"),
        P("adapter"),
        P(("replica", "adapter"), "tensor", None, None),
        P(("replica", "adapter"), "tensor", None, None),
        P(("replica", "adapter"), None, "tensor", None),
        P(("replica", "adapter"), None, "tensor", None),
        P(("replica", "adapter")),
    )
    out_specs = P(("replica", "adapter"), None, "tensor")
    return jax.shard_map(
        per_device, mesh=mesh, in_specs=in_specs, out_specs=out_specs, check_vma=False
    )
```

time: 235 us -> 164 us (0.70)
  Pallas kernels: 22.7 us -> 147 us
  waiting for transfers between devices: 110 us -> 0 us
  local copies, waits for them, and re-layouts: 38.1 us -> 13.4 us
  other arithmetic: 22.5 us -> 3.69 us
  starting transfers between devices: 16.2 us -> 0 us
  between operations: 13.6 us -> 0.04 us
  matrix products: 9.85 us -> 0 us
    pallas_call x0 -> x1, Pallas kernels: none -> 147 us  [per_device(): pl.pallas_call(functools.partial(kernel, dims), out_shape=jax.ShapeDtypeS...]
    all_to_all x3 -> x0, waiting for transfers between devices: 79.2 us -> none  [the longest x1 45.6 us: per_device(): lax.all_to_all(expanded.reshape(accelerator_list, maximum_load, iteration...]
    psum x1 -> x0, waiting for transfers between devices: 31.1 us -> none  [per_device(): accumulated_total = lax.psum(partial_sum, 'tensor')]
    another operation x2 -> x0, Pallas kernels: 21.2 us -> none
    all_to_all x3 -> x0, starting transfers between devices: 16.2 us -> none  [the longest x1 6.32 us: per_device(): lax.all_to_all(labels, 'adapter', split_axis=0, concat_axis=0, tiled=True)]
    reshape x6 -> x0, local copies, waits for them, and re-layouts: 10.6 us -> none  [the longest x2 5.63 us: per_device(): merged_output.reshape(requests, iteration_total, embedding_dimension // h...]
    dot_general x4 -> x0, matrix products: 9.85 us -> none  [the longest x1 4.73 us: attend(): jnp.einsum('bpkgd,bqkd->bpkgq', grouped, fresh_keys, preferred_element_ty...]
    scatter x2 -> x0, local copies, waits for them, and re-layouts: 8.92 us -> none  [the longest x1 8.14 us: per_device(): outgoing = jnp.zeros((accelerator_list * maximum_load, iteration_total, e...]
  transfers between devices with their start and end apart: 4 -> 0, of which waited for: 3 -> 0; matrix products, arithmetic and copies ran while one was open for 11% -> 0% of each run, Pallas kernels for 1% -> 0%
where the time goes in v1:
time: 164 us
  Pallas kernels  147 us (90%)
  local copies, waits for them, and re-layouts  13.4 us (8%)
  other arithmetic  3.69 us (2%)
    pallas_call x1, Pallas kernels, per_device(): pl.pallas_call(functools.partial(kernel, dims), out_shape=jax.ShapeDtypeS...  147 us
    transpose x2, local copies, waits for them, and re-layouts, by_position(): return array.transpose(1, 0, 2).reshape(positions * reqs, width)  4.34 us

profile of v1, /device:TPU:0, one launch (start us, length us, event | category | flops | bytes accessed | tf_op | source)
XLA Modules:
  0.0 163.7 jit_solution(8941668806558060147)
XLA Ops:
  0.0 0.0 copy-start
  0.0 0.8 select_reduce_fusion
  0.9 0.2 convert_reduce_fusion
  1.1 0.6 and_select_fusion
  1.7 0.7 broadcast_reduce_fusion
  2.3 0.1 add.112
  2.4 0.1 add.114
  2.5 0.7 broadcast_in_dim.16
  3.2 0.7 broadcast_in_dim_reshape.3.gain_ref
  3.9 0.1 copy.38
  4.0 0.1 copy.33
  4.1 0.6 fusion.6.pos_col_ref
  4.7 0.9 copy.47
  5.7 0.9 copy.46
  6.6 0.5 fusion
  7.2 0.9 pad_maximum_fusion
  8.0 0.9 pad.8.fresh_value_hbm
  8.9 0.9 pad.7.fresh_key_hbm
  9.8 2.8 %copy.39 = bf16[4,64,2048]{2,1,0:T(8,128)(2,1)} copy(bf16[4,64,2048]{2,0,1:T(4,128)(2,1)} %bitcast.41) | data formatting | bytes 2097152 | tf_op jit(solution)/shard_map/transpose | solution.py:327
  12.6 0.0 copy-done
  12.6 1.6 copy.40
  14.1 146.5 %shard_map.118 = bf16[4,64,2048]{2,1,0:T(8,128)(2,1)} custom-call(s32[64]{0:T(128)} %len_ref.1, s32[1,64]{1,0:T(1,128)} %get-tuple-element.9.pos_ref, s32[64,1]{1,0:T(8,128)} %fusion.6.pos_col_ref, s32[1,64]{1,0:T(1,128)} %get-tuple-element.8.slot_ref, f32[1,512]{1,0:T(1,128)} %broadcast_in_dim_reshape.3.gain_ref, bf16[256,2048]{1,0:T(8,128)(2,1)} %bitcast.37, ...), custom_call_target="tpu_custom_call" | custom-call | flops 3221225472 | bytes 16777216 | tf_op jit(solution)/shard_map/pallas_call | solution.py:339
  160.7 3.0 %copy.43 = bf16[64,4,2048]{2,1,0:T(4,128)(2,1)} copy(bf16[64,4,2048]{2,0,1:T(8,128)(2,1)} %bitcast.36) | data formatting | bytes 2097152 | tf_op jit(solution)/shard_map/transpose | solution.py:390
  (4 shorter events, 0.0 us)
Async XLA Ops:
  0.0 12.6 %copy-start = (bf16[64,4,2048]{2,1,0:T(4,128)(2,1)S(1)}, bf16[64,4,2048]{2,1,0:T(4,128)(2,1)}, u32[]{:S(2)}) copy-start(bf16[64,4,2048]{2,1,0:T(4,128)(2,1)} %param.13) | copy-start | bytes 3145732

commit v2 on v1

--- a/solution.py
+++ b/solution.py
@@ -238,27 +238,37 @@
     new_valid = (lane >= context) & (lane - context <= at)
     scaling = 128 ** (-0.5)
 
-    def attend(r):
-        old_valid = lane < jnp.minimum(len_ref[r], context)
-        valid = old_valid | new_valid
-        for g in range(kv):
-            span = pl.ds(pl.multiple_of(r * row_count + g * queries, queries), queries)
-            query = rows[span, :].astype(jnp.bfloat16)
-            scores = nt_dot(query, keys[r, g]) * scaling
-            scores = jnp.where(valid, scores, -jnp.inf)
-            top = jnp.max(scores, axis=1, keepdims=True)
-            weights = jnp.exp(scores - top)
-            weights = weights / jnp.sum(weights, axis=1, keepdims=True)
-            rows[span, :] = jnp.dot(
-                weights.astype(jnp.bfloat16), values[r, g], preferred_element_type=jnp.float32
-            )
-
-    def attend_some(b, _):
-        for i in range(4):
-            attend(b * 4 + i)
+    together = 4
+
+    def attend(b, _):
+        pairs = [(b * together + i, g) for i in range(together) for g in range(kv)]
+        spans = [
+            pl.ds(pl.multiple_of(r * row_count + g * queries, queries), queries) for r, g in pairs
+        ]
+        valid = [
+            (lane < jnp.minimum(len_ref[b * together + i], context)) | new_valid
+            for i in range(together)
+        ]
+        scores = [
+            nt_dot(rows[span, :].astype(jnp.bfloat16), keys[r, g])
+            for span, (r, g) in zip(spans, pairs)
+        ]
+        scores = [
+            jnp.where(valid[i // kv], score * scaling, -jnp.inf) for i, score in enumerate(scores)
+        ]
+        tops = [jnp.max(score, axis=1, keepdims=True) for score in scores]
+        weights = [jnp.exp(score - top) for score, top in zip(scores, tops)]
+        sums = [jnp.sum(weight, axis=1, keepdims=True) for weight in weights]
+        weights = [(weight / s).astype(jnp.bfloat16) for weight, s in zip(weights, sums)]
+        results = [
+            jnp.dot(weight, values[r, g], preferred_element_type=jnp.float32)
+            for weight, (r, g) in zip(weights, pairs)
+        ]
+        for span, result in zip(spans, results):
+            rows[span, :] = result
         return 0
 
-    lax.fori_loop(0, reqs // 4, attend_some, 0)
+    lax.fori_loop(0, reqs // together, attend, 0)
 
     def finish(p, _):
         for h in range(heads):

time: 164 us -> 130 us (0.79)
  Pallas kernels: 147 us -> 113 us
    pallas_call x1, Pallas kernels: 147 us -> 113 us  [per_device(): pl.pallas_call(functools.partial(kernel, dims), out_shape=jax.ShapeDtypeS...]
where the time goes in v2:
time: 130 us
  Pallas kernels  113 us (87%)
  local copies, waits for them, and re-layouts  13.4 us (10%)
  other arithmetic  3.69 us (3%)
    pallas_call x1, Pallas kernels, per_device(): pl.pallas_call(functools.partial(kernel, dims), out_shape=jax.ShapeDtypeS...  113 us
    transpose x2, local copies, waits for them, and re-layouts, by_position(): return array.transpose(1, 0, 2).reshape(positions * reqs, width)  4.34 us
    transpose x1, local copies, waits for them, and re-layouts, per_device(): return attended.transpose(1, 0, 2)  3.01 us

profile of v2, /device:TPU:0, one launch (start us, length us, event | category | flops | bytes accessed | tf_op | source)
XLA Modules:
  0.0 129.7 jit_solution(12944261095584620417)
XLA Ops:
  0.0 0.0 copy-start
  0.0 0.8 select_reduce_fusion
  0.9 0.2 convert_reduce_fusion
  1.1 0.6 and_select_fusion
  1.7 0.7 broadcast_reduce_fusion
  2.3 0.1 add.112
  2.4 0.1 add.114
  2.5 0.7 broadcast_in_dim.16
  3.2 0.7 broadcast_in_dim_reshape.3.gain_ref
  3.9 0.1 copy.38
  4.0 0.1 copy.33
  4.1 0.6 fusion.6.pos_col_ref
  4.7 0.9 copy.47
  5.7 0.9 copy.46
  6.6 0.5 fusion
  7.2 0.9 pad_maximum_fusion
  8.0 0.9 pad.8.fresh_value_hbm
  8.9 0.9 pad.7.fresh_key_hbm
  9.8 2.8 %copy.39 = bf16[4,64,2048]{2,1,0:T(8,128)(2,1)} copy(bf16[4,64,2048]{2,0,1:T(4,128)(2,1)} %bitcast.41) | data formatting | bytes 2097152 | tf_op jit(solution)/shard_map/transpose | solution.py:337
  12.6 0.0 copy-done
  12.6 1.6 %copy.40 = bf16[4,64,2048]{2,1,0:T(8,128)(2,1)} copy(bf16[4,64,2048]{2,0,1:T(4,128)(2,1)S(1)} %bitcast.42) | data formatting | bytes 2097152 | tf_op jit(solution)/shard_map/transpose | solution.py:337
  14.1 112.6 %shard_map.118 = bf16[4,64,2048]{2,1,0:T(8,128)(2,1)} custom-call(s32[64]{0:T(128)} %len_ref.1, s32[1,64]{1,0:T(1,128)} %get-tuple-element.9.pos_ref, s32[64,1]{1,0:T(8,128)} %fusion.6.pos_col_ref, s32[1,64]{1,0:T(1,128)} %get-tuple-element.8.slot_ref, f32[1,512]{1,0:T(1,128)} %broadcast_in_dim_reshape.3.gain_ref, bf16[256,2048]{1,0:T(8,128)(2,1)} %bitcast.37, ...), custom_call_target="tpu_custom_call" | custom-call | flops 3221225472 | bytes 16777216 | tf_op jit(solution)/shard_map/pallas_call | solution.py:349
  126.7 3.0 %copy.43 = bf16[64,4,2048]{2,1,0:T(4,128)(2,1)} copy(bf16[64,4,2048]{2,0,1:T(8,128)(2,1)} %bitcast.36) | data formatting | bytes 2097152 | tf_op jit(solution)/shard_map/transpose | solution.py:400
  (4 shorter events, 0.0 us)
Async XLA Ops:
  0.0 12.6 %copy-start = (bf16[64,4,2048]{2,1,0:T(4,128)(2,1)S(1)}, bf16[64,4,2048]{2,1,0:T(4,128)(2,1)}, u32[]{:S(2)}) copy-start(bf16[64,4,2048]{2,1,0:T(4,128)(2,1)} %param.13) | copy-start | bytes 3145732

commit v3 on v2

--- a/solution.py
+++ b/solution.py
@@ -24,10 +24,11 @@
 def kernel(
     dims,
     len_ref,
-    pos_ref,
-    pos_col_ref,
-    slot_ref,
     gain_ref,
+    ids_ref,
+    home_ref,
+    len_row_ref,
+    frequency_ref,
     hidden_hbm,
     uq_hbm,
     down_hbm,
@@ -36,11 +37,12 @@
     value_hbm,
     fresh_key_hbm,
     fresh_value_hbm,
-    cos_ref,
-    sin_ref,
     out_ref,
     hidden,
     uq,
+    uq_rows,
+    cosines,
+    sines,
     down,
     up,
     keys,
@@ -63,7 +65,7 @@
     back_send,
     back_recv,
 ):
-    n, tensors, chunks, cap, reqs, positions, context = dims
+    n, tensors, chunks, cap, reqs, positions, context, slots_dev = dims
     per = positions // chunks
     block = per * cap
     total = n * block
@@ -90,13 +92,14 @@
         pltpu.make_async_copy(uq_hbm, uq, local_sems.at[3]),
         pltpu.make_async_copy(key_hbm, keys.at[:, :, pl.ds(0, context), :], local_sems.at[4]),
         pltpu.make_async_copy(value_hbm, values.at[:, :, pl.ds(0, context), :], local_sems.at[5]),
-        pltpu.make_async_copy(
-            fresh_key_hbm, keys.at[:, :, pl.ds(context, 16), :], local_sems.at[6]
-        ),
-        pltpu.make_async_copy(
-            fresh_value_hbm, values.at[:, :, pl.ds(context, 16), :], local_sems.at[7]
-        ),
     ]
+    for g in range(kv):
+        for i, (fresh_hbm, cache) in enumerate(((fresh_key_hbm, keys), (fresh_value_hbm, values))):
+            loads.append(
+                pltpu.make_async_copy(
+                    fresh_hbm, cache.at[:, g, pl.ds(context, 16), :], local_sems.at[6 + 2 * g + i]
+                )
+            )
     for load in loads:
         load.start()
 
@@ -138,8 +141,25 @@
         slot = row & (cap - 1)
         return (pos == peer * cap + slot) & (row_pos == (col >> log2(reqs)))
 
-    forward = pick((total, per * reqs), 0, pos_ref[...])
-    label_rows = jnp.sum(jnp.where(forward, slot_ref[...], 0), axis=1, keepdims=True)
+    def as_column(row):
+        size = row.shape[1]
+        down_axis = lax.broadcasted_iota(jnp.int32, (size, size), 0)
+        diagonal = down_axis == lax.broadcasted_iota(jnp.int32, (size, size), 1)
+        return jnp.sum(jnp.where(diagonal, row, 0), axis=1, keepdims=True)
+
+    span = per * reqs
+    home_column = as_column(home_ref[...])
+    table = lax.broadcasted_iota(jnp.int32, (home_column.shape[0], span), 0)
+    home_slot = jnp.sum(jnp.where(table == ids_ref[...], home_column, 0), axis=0, keepdims=True)
+    hop = ((home_slot >> log2(slots_dev)) - me + n) & (n - 1)
+    local_slot = home_slot & (slots_dev - 1)
+    other = lax.broadcasted_iota(jnp.int32, (span, span), 0)
+    this = lax.broadcasted_iota(jnp.int32, (span, span), 1) & (reqs - 1)
+    earlier = (as_column(hop) == hop) & (other < this)
+    pos = hop * cap + jnp.sum(jnp.where(earlier, 1, 0), axis=0, keepdims=True)
+
+    forward = pick((total, span), 0, pos)
+    label_rows = jnp.sum(jnp.where(forward, local_slot, 0), axis=1, keepdims=True)
     label_rows = jnp.broadcast_to(label_rows, (total, 128)).reshape(n, block, 128)
     labels_out[...] = label_rows
     labels_in[0] = label_rows[0]
@@ -150,17 +170,30 @@
     for k in range(1, n):
         label_copy(k).start()
 
-    def dispatch(c, _):
-        source = hidden[pl.ds(pl.multiple_of(c * per * reqs, per * reqs), per * reqs), :]
-        sent = jnp.dot(forward, source, preferred_element_type=jnp.float32)
+    def position_rows(ref, c):
+        pieces = [ref[:, c * per + i, :] for i in range(per)]
+        return pieces[0] if per == 1 else jnp.concatenate(pieces, axis=0)
+
+    for c in range(chunks):
+        sent = jnp.dot(forward, position_rows(hidden, c), preferred_element_type=jnp.float32)
         sent = sent.astype(jnp.bfloat16).reshape(n, block, width)
         outgoing[c] = sent
         arrived[c, 0] = sent[0]
         for k in range(1, n):
             out_copy(c, k).start()
-        return 0
-
-    lax.fori_loop(0, chunks, dispatch, 0)
+
+    backward = pick((span, total), 1, as_column(pos))
+    backward = jnp.where(backward, 1.0, 0.0).astype(jnp.bfloat16)
+    lengths = as_column(len_row_ref[...])
+    low_half = lax.broadcasted_iota(jnp.int32, (reqs, 128), 1) < 64
+    for p in range(positions):
+        angles = (lengths + p).astype(jnp.float32) * frequency_ref[...]
+        cosines[pl.ds(p * reqs, reqs), :] = jnp.cos(angles)
+        sine = jnp.sin(angles)
+        sines[pl.ds(p * reqs, reqs), :] = jnp.where(low_half, -sine, sine)
+    loads[3].wait()
+    for c in range(chunks):
+        uq_rows[pl.ds(c * span, span), :] = position_rows(uq, c)
     for k in range(1, n):
         label_copy(k).wait()
     loads[1].wait()
@@ -193,7 +226,7 @@
         )
         pieces = []
         for j in range(groups):
-            scaled = both * gain_ref[:, j * 128 : (j + 1) * 128]
+            scaled = both * jnp.where(lane >= 64, gain_ref[2 * j + 1], gain_ref[2 * j])
             pieces.append(jnp.where(label == 2 * j + odd, scaled, 0.0).astype(jnp.bfloat16))
         shrunk = jnp.concatenate(pieces, axis=1)
         expanded = jnp.dot(shrunk, up[...], preferred_element_type=jnp.float32)
@@ -206,20 +239,16 @@
 
     lax.fori_loop(0, chunks, work, 0)
 
-    backward = pick((per * reqs, total), 1, pos_col_ref[...])
-    backward = jnp.where(backward, 1.0, 0.0).astype(jnp.bfloat16)
-    loads[3].wait()
-
     def combine(c, _):
         for k in range(1, n):
             back_copy(c, k).wait_recv()
-        span = pl.ds(pl.multiple_of(c * per * reqs, per * reqs), per * reqs)
+        part_rows = pl.ds(pl.multiple_of(c * span, span), span)
         delta = jnp.dot(
             backward, returned[c].reshape(total, width), preferred_element_type=jnp.float32
         )
-        merged = uq[span, :].astype(jnp.float32) + delta
-        cosine = cos_ref[span, :]
-        sine = sin_ref[span, :]
+        merged = uq_rows[part_rows, :].astype(jnp.float32) + delta
+        cosine = cosines[part_rows, :]
+        sine = sines[part_rows, :]
         for h in range(heads):
             part = merged[:, h * 128 : (h + 1) * 128]
             part = part * cosine + pltpu.roll(part, 64, 1) * sine
@@ -235,10 +264,12 @@
     queries = positions * group
     lane = lax.broadcasted_iota(jnp.int32, (queries, context + 16), 1)
     at = lax.broadcasted_iota(jnp.int32, (queries, context + 16), 0) >> log2(group)
-    new_valid = (lane >= context) & (lane - context <= at)
+    new_at = (lane - context) >> log2(kv)
+    new_head = (lane - context) & (kv - 1)
+    new_valid = [(lane >= context) & (new_at <= at) & (new_head == g) for g in range(kv)]
     scaling = 128 ** (-0.5)
 
-    together = 4
+    together = 8
 
     def attend(b, _):
         pairs = [(b * together + i, g) for i in range(together) for g in range(kv)]
@@ -246,15 +277,14 @@
             pl.ds(pl.multiple_of(r * row_count + g * queries, queries), queries) for r, g in pairs
         ]
         valid = [
-            (lane < jnp.minimum(len_ref[b * together + i], context)) | new_valid
-            for i in range(together)
+            (lane < jnp.minimum(len_ref[r], context)) | new_valid[g] for r, g in pairs
         ]
         scores = [
             nt_dot(rows[span, :].astype(jnp.bfloat16), keys[r, g])
             for span, (r, g) in zip(spans, pairs)
         ]
         scores = [
-            jnp.where(valid[i // kv], score * scaling, -jnp.inf) for i, score in enumerate(scores)
+            jnp.where(valid[i], score * scaling, -jnp.inf) for i, score in enumerate(scores)
         ]
         tops = [jnp.max(score, axis=1, keepdims=True) for score in scores]
         weights = [jnp.exp(score - top) for score, top in zip(scores, tops)]
@@ -304,7 +334,6 @@
 ):
     n = lax.axis_size("adapter")
     tensors = lax.axis_size("tensor")
-    me = lax.axis_index("adapter")
     reqs, positions, width = hidden.shape
     slots_dev, _, rank = reduce_matrices.shape
     kv, context, head_dim = key_cache.shape[1:]
@@ -314,34 +343,18 @@
     per = positions // chunks
     block = per * cap
     total = n * block
-    matches = adapter_ids[:, None] == jnp.arange(adapter_home.shape[0], dtype=jnp.int32)[None, :]
-    home_slot = jnp.sum(jnp.where(matches, adapter_home[None, :], 0), axis=1)
-    hop = lax.rem(home_slot // slots_dev - me + n, n)
-    local_slot = home_slot % slots_dev
-    order = jnp.arange(reqs, dtype=jnp.int32)
-    earlier = (hop[:, None] == hop[None, :]) & (order[None, :] < order[:, None])
-    pos = hop * cap + jnp.sum(earlier.astype(jnp.int32), axis=1)
-    pos = jnp.tile(pos, per)
-    slot_row = jnp.tile(local_slot, per)[None, :]
-    gain_row = jnp.repeat(correction_gain_table, rank)[None, :]
-
     half = head_dim // 2
     frequency = rope_theta ** (-2.0 * jnp.arange(half, dtype=jnp.float32) / head_dim)
-    offsets = cache_len[None, :] + jnp.arange(positions, dtype=jnp.int32)[:, None]
-    angles = offsets.astype(jnp.float32)[:, :, None] * frequency[None, None, :]
-    cosine, sine = jnp.cos(angles), jnp.sin(angles)
-    cosine = jnp.concatenate([cosine, cosine], axis=-1).reshape(positions * reqs, head_dim)
-    sine = jnp.concatenate([-sine, sine], axis=-1).reshape(positions * reqs, head_dim)
-
-    def by_position(array):
-        return array.transpose(1, 0, 2).reshape(positions * reqs, width)
+    frequency = jnp.concatenate([frequency, frequency])[None, :]
 
     def fresh(array):
-        return jnp.pad(array.transpose(0, 2, 1, 3), ((0, 0), (0, 0), (0, 16 - positions), (0, 0)))
+        return jnp.pad(
+            array.reshape(reqs, positions * kv, head_dim), ((0, 0), (0, 16 - positions * kv), (0, 0))
+        )
 
     down = reduce_matrices.transpose(0, 2, 1).reshape(slots_dev * rank, width)
     up = expand_matrices.reshape(slots_dev * rank, width)
-    dims = (n, tensors, chunks, cap, reqs, positions, context)
+    dims = (n, tensors, chunks, cap, reqs, positions, context, slots_dev)
     bf16, f32 = jnp.bfloat16, jnp.float32
     dma = pltpu.SemaphoreType.DMA
     vmem = pl.BlockSpec(memory_space=pltpu.VMEM)
@@ -349,11 +362,14 @@
     attended = pl.pallas_call(
         functools.partial(kernel, dims),
         out_shape=jax.ShapeDtypeStruct((positions, reqs, width), bf16),
-        in_specs=[pl.BlockSpec(memory_space=pltpu.SMEM)] + [vmem] * 4 + [whole] * 8 + [vmem] * 2,
+        in_specs=[pl.BlockSpec(memory_space=pltpu.SMEM)] * 2 + [vmem] * 4 + [whole] * 8,
         out_specs=vmem,
         scratch_shapes=[
+            pltpu.VMEM((reqs, positions, width), bf16),
+            pltpu.VMEM((reqs, positions, width), bf16),
             pltpu.VMEM((positions * reqs, width), bf16),
-            pltpu.VMEM((positions * reqs, width), bf16),
+            pltpu.VMEM((positions * reqs, head_dim), f32),
+            pltpu.VMEM((positions * reqs, head_dim), f32),
             pltpu.VMEM(down.shape, bf16),
             pltpu.VMEM(up.shape, bf16),
             pltpu.VMEM((reqs, kv, context + 16, head_dim), bf16),
@@ -366,7 +382,7 @@
             pltpu.VMEM((chunks, n, block, width), bf16),
             pltpu.VMEM((chunks, n, block, width), bf16),
             pltpu.VMEM((reqs * positions * width // head_dim, head_dim), f32),
-            dma((8,)),
+            dma((6 + 2 * kv,)),
             dma((chunks, n)),
             dma((chunks, n)),
             dma((n,)),
@@ -382,20 +398,19 @@
         cost_estimate=pl.CostEstimate(flops=3 << 30, bytes_accessed=16 << 20, transcendentals=0),
     )(
         cache_len,
-        pos[None, :],
-        pos[:, None],
-        slot_row,
-        gain_row,
-        by_position(hidden),
-        by_position(unrotated_queries),
+        correction_gain_table,
+        jnp.tile(adapter_ids, per)[None, :],
+        adapter_home[None, :],
+        cache_len[None, :],
+        frequency,
+        hidden,
+        unrotated_queries,
         down,
         up,
         key_cache,
         value_cache,
         fresh(new_keys),
         fresh(new_values),
-        cosine,
-        sine,
     )
     return attended.transpose(1, 0, 2)
 

time: 130 us -> 117 us (0.900)
  local copies, waits for them, and re-layouts: 13.4 us -> 6.3 us
  other arithmetic: 3.69 us -> 0.64 us
  Pallas kernels: 113 us -> 110 us
    transpose x2 -> x0, local copies, waits for them, and re-layouts: 4.34 us -> none  [by_position(): return array.transpose(1, 0, 2).reshape(positions * reqs, width)]
    pallas_call x1, Pallas kernels: 113 us -> 110 us  [per_device(): pl.pallas_call(functools.partial(kernel, dims), out_shape=jax.ShapeDtypeS...]
    unnamed x4 -> x0, local copies, waits for them, and re-layouts: 1.89 us -> none
    pad x2, local copies, waits for them, and re-layouts: 1.77 us -> 3.3 us  [fresh(): jnp.pad(array.reshape(reqs, positions * kv, head_dim), ((0, 0), (0, 16 -...]
where the time goes in v3:
time: 117 us
  Pallas kernels  110 us (94%)
  local copies, waits for them, and re-layouts  6.3 us (5%)
    pallas_call x1, Pallas kernels, per_device(): pl.pallas_call(functools.partial(kernel, dims), out_shape=jax.ShapeDtypeS...  110 us
    pad x2, local copies, waits for them, and re-layouts, fresh(): jnp.pad(array.reshape(reqs, positions * kv, head_dim), ((0, 0), (0, 16 -...  3.3 us
    transpose x1, local copies, waits for them, and re-layouts, per_device(): return attended.transpose(1, 0, 2)  3.01 us

profile of v3, /device:TPU:0, one launch (start us, length us, event | category | flops | bytes accessed | tf_op | source)
XLA Modules:
  0.0 116.8 jit_solution(17501407997341502997)
XLA Ops:
  0.0 0.6 maximum_bitcast_fusion.frequency_ref
  0.6 1.6 %pad.7.fresh_key_hbm = bf16[64,16,128]{2,1,0:T(8,128)(2,1)} pad(bf16[64,8,128]{2,1,0:T(8,128)(2,1)} %bitcast.15, bf16[]{:T(256)} %constant.9.clone.1), padding=0_0x0_8x0_0 | pad | bytes 393218 | tf_op jit(solution)/shard_map/jit(_pad)/pad | solution.py:351
  2.3 1.7 %pad.8.fresh_value_hbm = bf16[64,16,128]{2,1,0:T(8,128)(2,1)} pad(bf16[64,8,128]{2,1,0:T(8,128)(2,1)} %bitcast.16, bf16[]{:T(256)} %constant.9.clone.1), padding=0_0x0_8x0_0 | pad | bytes 393218 | tf_op jit(solution)/shard_map/jit(_pad)/pad | solution.py:351
  3.9 109.8 %shard_map.118 = bf16[4,64,2048]{2,1,0:T(8,128)(2,1)} custom-call(s32[64]{0:T(128)} %len_ref.1, f32[8]{0:T(128)} %gain_ref.1, s32[1,64]{1,0:T(1,128)} %bitcast.18, s32[1,32]{1,0:T(1,128)} %bitcast.19, s32[1,64]{1,0:T(1,128)} %bitcast.17, f32[1,128]{1,0:T(1,128)} %maximum_bitcast_fusion.frequency_ref, bf16[64,4,2048]{2,1,0:T(4,128)(2,1)} %hidden_hbm.1, ...), custom_call_target="tpu_custom_call" | custom-call | flops 3221225472 | bytes 16777216 | tf_op jit(solution)/shard_map/pallas_call | solution.py:362
  113.8 3.0 %copy.13 = bf16[64,4,2048]{2,1,0:T(4,128)(2,1)} copy(bf16[64,4,2048]{2,0,1:T(8,128)(2,1)} %bitcast.12) | data formatting | bytes 2097152 | tf_op jit(solution)/shard_map/transpose | solution.py:415
  (1 shorter events, 0.0 us)

commit v4 on v3

--- a/solution.py
+++ b/solution.py
@@ -47,6 +47,8 @@
     up,
     keys,
     values,
+    fresh_keys,
+    fresh_values,
     outgoing,
     arrived,
     labels_out,
@@ -92,16 +94,10 @@
         pltpu.make_async_copy(uq_hbm, uq, local_sems.at[3]),
         pltpu.make_async_copy(key_hbm, keys.at[:, :, pl.ds(0, context), :], local_sems.at[4]),
         pltpu.make_async_copy(value_hbm, values.at[:, :, pl.ds(0, context), :], local_sems.at[5]),
+        pltpu.make_async_copy(fresh_key_hbm, fresh_keys, local_sems.at[6]),
+        pltpu.make_async_copy(fresh_value_hbm, fresh_values, local_sems.at[7]),
     ]
-    for g in range(kv):
-        for i, (fresh_hbm, cache) in enumerate(((fresh_key_hbm, keys), (fresh_value_hbm, values))):
-            loads.append(
-                pltpu.make_async_copy(
-                    fresh_hbm, cache.at[:, g, pl.ds(context, 16), :], local_sems.at[6 + 2 * g + i]
-                )
-            )
-    for load in loads:
-        load.start()
+    loads[0].start()
 
     barrier = pltpu.get_barrier_semaphore()
     for k in range(1, n):
@@ -169,6 +165,8 @@
     pl.semaphore_wait(barrier, n - 1 + tensors - 1)
     for k in range(1, n):
         label_copy(k).start()
+    for load in loads[1:3]:
+        load.start()
 
     def position_rows(ref, c):
         pieces = [ref[:, c * per + i, :] for i in range(per)]
@@ -181,6 +179,9 @@
         arrived[c, 0] = sent[0]
         for k in range(1, n):
             out_copy(c, k).start()
+
+    for load in loads[3:]:
+        load.start()
 
     backward = pick((span, total), 1, as_column(pos))
     backward = jnp.where(backward, 1.0, 0.0).astype(jnp.bfloat16)
@@ -194,6 +195,14 @@
     loads[3].wait()
     for c in range(chunks):
         uq_rows[pl.ds(c * span, span), :] = position_rows(uq, c)
+    for load in loads[6:]:
+        load.wait()
+    for fresh, cache in ((fresh_keys, keys), (fresh_values, values)):
+        given = fresh[...].astype(jnp.float32)
+        blank = jnp.zeros((reqs, 16 - given.shape[1], 128), jnp.float32)
+        padded = jnp.concatenate([given, blank], axis=1).astype(jnp.bfloat16)
+        for g in range(kv):
+            cache[:, g, context : context + 16, :] = padded
     for k in range(1, n):
         label_copy(k).wait()
     loads[1].wait()
@@ -202,6 +211,12 @@
     def work(c, _):
         for k in range(1, n):
             out_copy(c, k).wait_recv()
+
+        @pl.when(c > 0)
+        def _():
+            for k in range(1, n):
+                back_copy(c - 1, k).start()
+
         label = labels_in[...].reshape(total, 128)
         lane = lax.broadcasted_iota(jnp.int32, (total, 128), 1)
         odd = jnp.where(lane >= 64, 1, 0)
@@ -233,11 +248,11 @@
         expanded = expanded.astype(jnp.bfloat16).reshape(n, block, width)
         returning[c] = expanded
         returned[c, 0] = expanded[0]
-        for k in range(1, n):
-            back_copy(c, k).start()
         return 0
 
     lax.fori_loop(0, chunks, work, 0)
+    for k in range(1, n):
+        back_copy(chunks - 1, k).start()
 
     def combine(c, _):
         for k in range(1, n):
@@ -257,48 +272,54 @@
                 rows[pl.ds(first, reqs, stride=row_count), :] = part[i * reqs : (i + 1) * reqs]
         return 0
 
-    lax.fori_loop(0, chunks, combine, 0)
-    for load in loads[4:]:
+    def attend_positions(begin, end):
+        queries = (end - begin) * group
+        lane = lax.broadcasted_iota(jnp.int32, (queries, context + 16), 1)
+        at = (lax.broadcasted_iota(jnp.int32, lane.shape, 0) >> log2(group)) + begin
+        new_at = (lane - context) >> log2(kv)
+        new_head = (lane - context) & (kv - 1)
+        new_valid = [(lane >= context) & (new_at <= at) & (new_head == g) for g in range(kv)]
+        scaling = 128 ** (-0.5)
+
+        together = 8
+
+        def attend(b, _):
+            pairs = [(b * together + i, g) for i in range(together) for g in range(kv)]
+            spans = [
+                pl.ds(pl.multiple_of(r * row_count + (g * positions + begin) * group, group), queries) for r, g in pairs
+            ]
+            valid = [
+                (lane < jnp.minimum(len_ref[r], context)) | new_valid[g] for r, g in pairs
+            ]
+            scores = [
+                nt_dot(rows[span, :].astype(jnp.bfloat16), keys[r, g])
+                for span, (r, g) in zip(spans, pairs)
+            ]
+            scores = [
+                jnp.where(valid[i], score * scaling, -jnp.inf) for i, score in enumerate(scores)
+            ]
+            tops = [jnp.max(score, axis=1, keepdims=True) for score in scores]
+            weights = [jnp.exp(score - top) for score, top in zip(scores, tops)]
+            sums = [jnp.sum(weight, axis=1, keepdims=True) for weight in weights]
+            weights = [(weight / s).astype(jnp.bfloat16) for weight, s in zip(weights, sums)]
+            results = [
+                jnp.dot(weight, values[r, g], preferred_element_type=jnp.float32)
+                for weight, (r, g) in zip(weights, pairs)
+            ]
+            for span, result in zip(spans, results):
+                rows[span, :] = result
+            return 0
+
+        lax.fori_loop(0, reqs // together, attend, 0)
+
+    early = max(0, positions - 1) if chunks == positions else 0
+    lax.fori_loop(0, early, combine, 0)
+    for load in loads[4:6]:
         load.wait()
-
-    queries = positions * group
-    lane = lax.broadcasted_iota(jnp.int32, (queries, context + 16), 1)
-    at = lax.broadcasted_iota(jnp.int32, (queries, context + 16), 0) >> log2(group)
-    new_at = (lane - context) >> log2(kv)
-    new_head = (lane - context) & (kv - 1)
-    new_valid = [(lane >= context) & (new_at <= at) & (new_head == g) for g in range(kv)]
-    scaling = 128 ** (-0.5)
-
-    together = 8
-
-    def attend(b, _):
-        pairs = [(b * together + i, g) for i in range(together) for g in range(kv)]
-        spans = [
-            pl.ds(pl.multiple_of(r * row_count + g * queries, queries), queries) for r, g in pairs
-        ]
-        valid = [
-            (lane < jnp.minimum(len_ref[r], context)) | new_valid[g] for r, g in pairs
-        ]
-        scores = [
-            nt_dot(rows[span, :].astype(jnp.bfloat16), keys[r, g])
-            for span, (r, g) in zip(spans, pairs)
-        ]
-        scores = [
-            jnp.where(valid[i], score * scaling, -jnp.inf) for i, score in enumerate(scores)
-        ]
-        tops = [jnp.max(score, axis=1, keepdims=True) for score in scores]
-        weights = [jnp.exp(score - top) for score, top in zip(scores, tops)]
-        sums = [jnp.sum(weight, axis=1, keepdims=True) for weight in weights]
-        weights = [(weight / s).astype(jnp.bfloat16) for weight, s in zip(weights, sums)]
-        results = [
-            jnp.dot(weight, values[r, g], preferred_element_type=jnp.float32)
-            for weight, (r, g) in zip(weights, pairs)
-        ]
-        for span, result in zip(spans, results):
-            rows[span, :] = result
-        return 0
-
-    lax.fori_loop(0, reqs // together, attend, 0)
+    if early:
+        attend_positions(0, early)
+    lax.fori_loop(early, chunks, combine, 0)
+    attend_positions(early, positions)
 
     def finish(p, _):
         for h in range(heads):
@@ -348,9 +369,7 @@
     frequency = jnp.concatenate([frequency, frequency])[None, :]
 
     def fresh(array):
-        return jnp.pad(
-            array.reshape(reqs, positions * kv, head_dim), ((0, 0), (0, 16 - positions * kv), (0, 0))
-        )
+        return array.reshape(reqs, positions * kv, head_dim)
 
     down = reduce_matrices.transpose(0, 2, 1).reshape(slots_dev * rank, width)
     up = expand_matrices.reshape(slots_dev * rank, width)
@@ -374,6 +393,8 @@
             pltpu.VMEM(up.shape, bf16),
             pltpu.VMEM((reqs, kv, context + 16, head_dim), bf16),
             pltpu.VMEM((reqs, kv, context + 16, head_dim), bf16),
+            pltpu.VMEM((reqs, positions * kv, head_dim), bf16),
+            pltpu.VMEM((reqs, positions * kv, head_dim), bf16),
             pltpu.VMEM((chunks, n, block, width), bf16),
             pltpu.VMEM((chunks, n, block, width), bf16),
             pltpu.VMEM((n, block, 128), jnp.int32),
@@ -382,7 +403,7 @@
             pltpu.VMEM((chunks, n, block, width), bf16),
             pltpu.VMEM((chunks, n, block, width), bf16),
             pltpu.VMEM((reqs * positions * width // head_dim, head_dim), f32),
-            dma((6 + 2 * kv,)),
+            dma((8,)),
             dma((chunks, n)),
             dma((chunks, n)),
             dma((n,)),

time: 117 us -> 113 us (0.966)
  local copies, waits for them, and re-layouts: 6.3 us -> 3.01 us
    pad x2 -> x0, local copies, waits for them, and re-layouts: 3.3 us -> none  [fresh(): jnp.pad(array.reshape(reqs, positions * kv, head_dim), ((0, 0), (0, 16 -...]
where the time goes in v4:
time: 113 us; the launch traced here: 112 us
  Pallas kernels  109 us (96%)
  local copies, waits for them, and re-layouts  3.01 us (3%)
    pallas_call x1, Pallas kernels, per_device(): pl.pallas_call(functools.partial(kernel, dims), out_shape=jax.ShapeDtypeS...  109 us
    transpose x1, local copies, waits for them, and re-layouts, per_device(): return attended.transpose(1, 0, 2)  3.01 us

profile of v4, /device:TPU:0, one launch (start us, length us, event | category | flops | bytes accessed | tf_op | source)
XLA Modules:
  0.0 112.4 jit_solution(7009008231869155432)
XLA Ops:
  0.0 0.6 maximum_bitcast_fusion.frequency_ref
  0.6 108.8 %shard_map.118 = bf16[4,64,2048]{2,1,0:T(8,128)(2,1)} custom-call(s32[64]{0:T(128)} %len_ref.1, f32[8]{0:T(128)} %gain_ref.1, s32[1,64]{1,0:T(1,128)} %bitcast.18, s32[1,32]{1,0:T(1,128)} %bitcast.19, s32[1,64]{1,0:T(1,128)} %bitcast.17, f32[1,128]{1,0:T(1,128)} %maximum_bitcast_fusion.frequency_ref, bf16[64,4,2048]{2,1,0:T(4,128)(2,1)} %hidden_hbm.1, ...), custom_call_target="tpu_custom_call" | custom-call | flops 3221225472 | bytes 16777216 | tf_op jit(solution)/shard_map/pallas_call | solution.py:381
  109.4 3.0 %copy.13 = bf16[64,4,2048]{2,1,0:T(4,128)(2,1)} copy(bf16[64,4,2048]{2,0,1:T(8,128)(2,1)} %bitcast.12) | data formatting | bytes 2097152 | tf_op jit(solution)/shard_map/transpose | solution.py:436
  (1 shorter events, 0.0 us)
